TPU v7x, 256 devices: a whole 4x4x8 slice. The times are simulated.
256 devices in a mesh: ctx: 4 (over y_hi, core), row: 8 (over x, y_lo), tp: 8 (over z).
Axes of the slice: x: 4, y: 4 (y_hi: 2, y_lo: 2; y = y_hi * 2 + y_lo), z: 8, core: 2. Of those that a mesh axis runs over, the one named last changes fastest.
Arguments:
- prefill_query: bfloat16 [8, 1024, 8192], P('row', 'ctx', 'tp')
- prefix_keys: bfloat16 [8, 8192, 1024], P('row', 'ctx', 'tp')
- prefix_values: bfloat16 [8, 8192, 1024], P('row', 'ctx', 'tp'), may hold values from -6 to 6
- span_keys: bfloat16 [8, 1024, 1024], P('row', 'ctx', 'tp'), may hold values from -6 to 6
- span_values: bfloat16 [8, 1024, 1024], P('row', 'ctx', 'tp'), may hold values from -6 to 6
- prefix_len: int32 [8], replicated, may hold values from 1 to 8192, as said below
- context_len: int32 [8], replicated, may hold values from 2 to 9216, as said below
- hidden: bfloat16 [256, 8192], P('tp', ('ctx', 'row'))
- qkv_weight: bfloat16 [8192, 8, 1280], P(('ctx', 'row'), 'tp')
- out_weight: bfloat16 [8192, 8192], P('tp', ('ctx', 'row'))
- cache_keys: bfloat16 [256, 1024, 1024], P(('ctx', 'row'), None, 'tp')
- cache_values: bfloat16 [256, 1024, 1024], P(('ctx', 'row'), None, 'tp'), may hold values from -6 to 6
- row_context: int32 [256], replicated, may hold values from 0 to 7
- cache_len: int32 [256], replicated, may hold values from 2 to 1024, as said below
Outputs:
- prefill_out: bfloat16 [8, 1024, 8192], P('row', 'ctx', 'tp')
- step_out: bfloat16 [2, 256, 8192], P(None, 'tp', ('ctx', 'row'))
Inputs may be any that keep to these rules, and one draw needn't show every extreme that they name: `prefix_len`: every context has at least one live slot before its block, and one context has all 8192. context_len - prefix_len is from 1 to 1024 for every context; the context that has all 8192 prefix slots also has a full block. `cache_len`: every proof row has at least two live cache slots; one row has all 1024.
All inputs are finite; a program needn't handle non-finite values.
Results may differ from a plain program's by a relative error of at most 0.04.
Values may be sent and summed in bfloat16 or wider, within the bound.
A program may use at most 128 MiB of HBM per device.

v0:
```python
import jax
import jax.numpy as jnp
from jax import lax
from jax.experimental import pallas as pl
from jax.experimental.pallas import tpu as pltpu
from jax.sharding import PartitionSpec as P

HD = 128
GROUP = 8
STEPS = 2
SPAN = 1024
CACHE = 1024
PIECE = 2048
DRW = 8
TAIL = 2 * SPAN
KEYS = TAIL + 128
UNIT = 1024
CHUNK = 256
NEGATIVE = -1e30
SCALE = HD ** (-0.5)
LOG2E = 1.4426950408889634
F32 = jnp.float32
BF16 = jnp.bfloat16
MESH = pl.DeviceIdType.MESH


def nt_dot(a, b):
    return lax.dot_general(a, b, (((1,), (1,)), ((), ())), preferred_element_type=F32)


def kernel(
    prefix_len, context_len, row_context, cache_len,
    q_hbm, pk_hbm, pv_hbm, sk_hbm, sv_hbm, hid_hbm, wq_hbm, wo_hbm, ck_hbm, cv_hbm,
    pre_out, step_out,
    q, kv, kx, vx, k0, span, kd, vd, bias, span_bias, wq, wo,
    state, xall, part, pair, rs_send, rs_recv, heads, new_kv, att_o, att_send, att_all, z_send, z_recv, late,
    m_ref, acc_ref,
    local_sem, z_ssem, z_rsem, pr_ssem, pr_rsem, rs_ssem, rs_rsem, at_ssem, at_rsem, fw_ssem, fw_rsem,
    rz_ssem, rz_rsem, k0_ssem, k0_rsem, s1_ssem, s1_rsem, s2_ssem, s2_rsem, sf_ssem, sf_rsem,
    pc_ssem, pc_rsem, pf_ssem, pf_rsem, pd_ssem, pd_rsem,
):
    ctx = lax.axis_index("ctx")
    row = lax.axis_index("row")
    tp = lax.axis_index("tp")
    core = ctx % 2
    y_hi = ctx // 2
    x = row // 2
    y_lo = row % 2
    y = y_hi * 2 + y_lo
    me = y_hi * 8 + row

    def plane(e):
        t = (me + e) % 16
        return t, {"ctx": (t // 8) * 2 + core, "row": t % 8}

    def along_y(e):
        t = (y + e) % 4
        return {"ctx": (t // 2) * 2 + core, "row": x * 2 + t % 2}

    def along_x(e):
        return {"row": ((x + e) % 4) * 2 + y_lo}

    def along_z(e):
        t = (tp + e) % 8
        return t, {"tp": t}

    other_core = {"ctx": y_hi * 2 + 1 - core}
    far = {"ctx": (1 - y_hi) * 2 + core}
    diagonal = {"ctx": (1 - y_hi) * 2 + 1 - core}
    other_ctx = y_hi * 2 + 1 - core
    far_ctx = (1 - y_hi) * 2 + core
    diagonal_ctx = (1 - y_hi) * 2 + 1 - core

    def remote(src, dst, ssem, rsem, device):
        return pltpu.make_async_remote_copy(
            src_ref=src, dst_ref=dst, send_sem=ssem, recv_sem=rsem, device_id=device, device_id_type=MESH
        )

    locals_ = [
        (hid_hbm.at[0], state.at[0]),
        (wq_hbm, wq),
        (pk_hbm, kv.at[ctx, 0]),
        (pv_hbm, kv.at[ctx, 1]),
        (sk_hbm, span.at[core, x, y, 0]),
        (sv_hbm, span.at[core, x, y, 1]),
        (q_hbm, q),
        (wo_hbm, wo),
        (ck_hbm, kd.at[:, pl.ds(SPAN, CACHE)]),
        (cv_hbm, vd.at[:, pl.ds(SPAN, CACHE)]),
        (pk_hbm.at[pl.ds(0, 16)], k0.at[ctx]),
    ]
    locals_ = [pltpu.make_async_copy(a, b, local_sem.at[i]) for i, (a, b) in enumerate(locals_)]
    for c in locals_:
        c.start()

    barrier = pltpu.get_barrier_semaphore()

    def greet(device):
        pl.semaphore_signal(barrier, inc=1, device_id=device, device_id_type=MESH)

    def greet_plane(e, _):
        greet(plane(e)[1])
        return 0

    def greet_z(e, _):
        greet(along_z(e)[1])
        return 0

    lax.fori_loop(1, 16, greet_plane, 0)
    lax.fori_loop(1, 8, greet_z, 0)
    greet(other_core)
    greet(diagonal)

    def hidden_copy(s, e):
        return remote(state.at[s], xall.at[s, tp], z_ssem.at[s, e], z_rsem.at[s, e], along_z(e)[1])

    def hidden_start(s):
        def body(e, _):
            hidden_copy(s, e).start()
            return 0
        lax.fori_loop(1, 8, body, 0)
        xall[s, tp] = state[s]

    def hidden_wait(s):
        def body(e, _):
            hidden_copy(s, e).wait()
            return 0
        lax.fori_loop(1, 8, body, 0)

    def pair_copy(s):
        return remote(part.at[s, 1 - core], pair.at[s], pr_ssem.at[s], pr_rsem.at[s], other_core)

    def rs_copy(s, e):
        t, device = plane(e)
        return remote(rs_send.at[s, t], rs_recv.at[s, me], rs_ssem.at[s, e], rs_rsem.at[s, e], device)

    def att_copy(s, e):
        return remote(att_send.at[s], att_all.at[s, core, me], at_ssem.at[s, e], at_rsem.at[s, e], plane(e)[1])

    def att_forward(s):
        return remote(att_all.at[s, core], att_all.at[s, core], fw_ssem.at[s], fw_rsem.at[s], other_core)

    def out_copy(s, e):
        t, device = along_z(e)
        block = ((t // 2) % 2 * 2 + t // 4) * 2 + t % 2
        return remote(z_send.at[s, block], z_recv.at[s, tp], rz_ssem.at[s, e], rz_rsem.at[s, e], device)

    k0_copies = [
        remote(k0.at[ctx], k0.at[ctx], k0_ssem.at[i], k0_rsem.at[i], device)
        for i, device in enumerate((other_core, far, diagonal))
    ]
    def span_first(e):
        piece = span.at[core, x, y]
        return (
            remote(piece, piece, s1_ssem.at[0, e], s1_rsem.at[0, e], along_x(e)),
            remote(piece, piece, s1_ssem.at[1, e], s1_rsem.at[1, e], along_y(e)),
        )

    def span_second(d, e):
        keys = span.at[core, (x + d) % 4, y, 0]
        values = span.at[core, x, (y + d) % 4, 1]
        return (
            remote(keys, keys, s2_ssem.at[0, d, e], s2_rsem.at[0, d, e], along_y(e)),
            remote(values, values, s2_ssem.at[1, d, e], s2_rsem.at[1, d, e], along_x(e)),
        )

    def span_core(d, e):
        piece = span.at[core, (x + d) % 4, (y + e) % 4]
        return remote(piece, piece, sf_ssem.at[d, e], sf_rsem.at[d, e], other_core)

    def span_open():
        for e in (1, 3, 2):
            for c in span_first(e):
                c.start()
        span_core(0, 0).start()

    def span_relay():
        for d in (1, 3, 2):
            along, across = span_first(d)
            along.wait()
            across.wait()
            for e in (1, 3, 2):
                for c in span_second(4 - d, e):
                    c.start()
            span_core(4 - d, 0).start()
            span_core(0, 4 - d).start()

    def span_own_ready():
        span_core(0, 0).wait()
        span_core(0, 2).wait()

    def span_close():
        for d in (1, 3, 2):
            for e in (1, 3, 2):
                for c in span_second(d, e):
                    c.wait()
        for d in (1, 2, 3):
            for e in (1, 2, 3):
                span_core(d, e).start()

    def span_done():
        for d in range(4):
            for e in range(4):
                if (d, e) not in ((0, 0), (0, 2)):
                    span_core(d, e).wait()

    prefix_core = remote(kv.at[ctx], kv.at[ctx], pc_ssem, pc_rsem, other_core)

    def prefix_far(i):
        chunk = kv.at[ctx, :, pl.ds(i * CHUNK, CHUNK)]
        return remote(chunk, chunk, pf_ssem.at[i], pf_rsem.at[i], far)

    def prefix_far_start(first, last):
        for i in range(first, last):
            prefix_far(i).start()

    def prefix_forward(j):
        half = kv.at[far_ctx, :, pl.ds(j * UNIT, UNIT)]
        return remote(half, half, pd_ssem.at[j], pd_rsem.at[j], other_core)

    def prefix_relay(j):
        per = UNIT // CHUNK
        for i in range(j * per, (j + 1) * per):
            prefix_far(i).wait()
        prefix_forward(j).start()

    def project(s):
        out = jnp.dot(xall[s].reshape(256, 256), wq[...], preferred_element_type=F32).reshape(32, 8, 1280)
        both = jnp.concatenate([out[:, :, :640], out[:, :, 640:]], 1).astype(BF16)
        for j in range(4):
            part[s, j % 2, pl.ds((j // 2) * 8, 8)] = both[j * 8:j * 8 + 8]
        pair_copy(s).start()

    def scatter(s):
        pair_copy(s).wait()
        rs_send[s] = (part[s, core].astype(F32) + pair[s].astype(F32)).astype(BF16)

        def body(e, _):
            rs_copy(s, e).start()
            return 0
        lax.fori_loop(1, 16, body, 0)
        rs_recv[s, me] = rs_send[s, me]

    def gather_rows(s):
        def body(e, _):
            rs_copy(s, e).wait()
            return 0
        lax.fori_loop(1, 16, body, 0)
        total = jnp.sum(rs_recv[s].astype(F32), 0).astype(BF16).astype(F32)
        for i in range(5):
            heads[i] = total[0:8, i * HD:(i + 1) * HD]
        for i in range(3):
            heads[5 + i] = total[8:16, i * HD:(i + 1) * HD]
        new_kv[s, 0] = total[8:16, 3 * HD:4 * HD]
        new_kv[s, 1] = total[8:16, 4 * HD:5 * HD]
        spot = lax.broadcasted_iota(jnp.int32, (16, HD), 0)
        for r in range(DRW):
            for which, buffer in ((0, kd), (1, vd)):
                fresh = jnp.zeros((16, HD), F32)
                for t in range(s + 1):
                    fresh = jnp.where(spot == t, new_kv[t, which, pl.ds(r, 1), :], fresh)
                buffer[r, pl.ds(TAIL, 16)] = fresh.astype(BF16)

    def query_rows():
        return jnp.stack([heads[:, r, :] for r in range(DRW)], 0).astype(BF16)

    def attend_cache():
        late[...] = lax.dot_general(
            query_rows(), kd[:, SPAN:KEYS], (((2,), (2,)), ((0,), (0,))), preferred_element_type=F32
        )

    def attend(s):
        early = lax.dot_general(
            query_rows(), kd[:, 0:SPAN], (((2,), (2,)), ((0,), (0,))), preferred_element_type=F32
        )
        scores = jnp.concatenate([early, late[...]], 2) * SCALE + bias[...]
        if s == 0:
            spot = lax.broadcasted_iota(jnp.int32, (DRW, GROUP, KEYS), 2)
            scores = jnp.where(spot == TAIL + 1, NEGATIVE, scores)
        peak = jnp.max(scores, -1, keepdims=True)
        expon = jnp.exp(scores - peak)
        total = jnp.sum(expon, -1, keepdims=True)
        summed = lax.dot_general(
            expon.astype(BF16), vd[...], (((2,), (1,)), ((0,), (0,))), preferred_element_type=F32
        )
        att_o[...] = summed / total
        for i in range(4):
            both = jnp.concatenate([att_o[:, i, :], att_o[:, 4 + i, :]], 0)
            att_send[s, :, i * HD:(i + 1) * HD] = both.astype(BF16)

        def body(e, _):
            att_copy(s, e).start()
            return 0
        lax.fori_loop(1, 16, body, 0)
        att_all[s, core, me] = att_send[s]

    def relay_attended(s):
        def body(e, _):
            att_copy(s, e).wait()
            return 0
        lax.fori_loop(1, 16, body, 0)
        att_forward(s).start()

    def out_project(s):
        att_forward(s).wait()
        rows = att_all[s].astype(F32).reshape(32, 16, 512)
        left = rows[:, 0:8].reshape(256, 512).astype(BF16)
        right = rows[:, 8:16].reshape(256, 512).astype(BF16)
        out = jnp.dot(left, wo[0:512], preferred_element_type=F32)
        out = out + jnp.dot(right, wo[512:1024], preferred_element_type=F32)
        z_send[s] = out.astype(BF16).reshape(8, 32, 256)

        def body(e, _):
            out_copy(s, e).start()
            return 0
        lax.fori_loop(1, 8, body, 0)
        z_recv[s, tp] = z_send[s, ((tp // 2) % 2 * 2 + tp // 4) * 2 + tp % 2]

    def finish_step(s):
        def body(e, _):
            out_copy(s, e).wait()
            return 0
        lax.fori_loop(1, 8, body, 0)
        result = jnp.sum(z_recv[s].astype(F32), 0).astype(BF16)
        step_out[s] = result
        if s + 1 < STEPS:
            state[s + 1] = (state[s].astype(F32) + result.astype(F32)).astype(BF16)

    def pick_span():
        def body(r, _):
            c = row_context[me_rows + r]
            for k in range(2):
                for h in range(2):
                    at = (h * 2 + k) * 256
                    kd[r, pl.ds(at, 256)] = span[k, c // 2, h * 2 + c % 2, 0]
                    vd[r, pl.ds(at, 256)] = span[k, c // 2, h * 2 + c % 2, 1]
            return 0
        lax.fori_loop(0, DRW, body, 0)

    me_rows = (ctx * 8 + row) * DRW

    def decode_bias():
        spot = lax.broadcasted_iota(jnp.int32, (GROUP, KEYS), 1)

        def body(r, _):
            c = row_context[me_rows + r]
            valid = context_len[c] - prefix_len[c]
            live = cache_len[me_rows + r]
            end = jnp.where(spot < SPAN, valid, jnp.where(spot < TAIL, SPAN + live, TAIL + STEPS))
            bias[r] = jnp.where(spot < end, 0.0, NEGATIVE)
            kd[r, pl.ds(TAIL, 128)] = jnp.zeros((128, HD), BF16)
            vd[r, pl.ds(TAIL, 128)] = jnp.zeros((128, HD), BF16)
            return 0
        lax.fori_loop(0, DRW, body, 0)

    def prefill_start():
        m_ref[...] = jnp.full(m_ref.shape, NEGATIVE, F32)
        acc_ref[...] = jnp.zeros(acc_ref.shape, F32)
        at = lax.broadcasted_iota(jnp.int32, (256, SPAN), 0) + ctx * 256
        spot = lax.broadcasted_iota(jnp.int32, (256, SPAN), 1)
        valid = context_len[row] - prefix_len[row]
        span_bias[...] = jnp.where((spot <= at) & (spot < valid), 0.0, NEGATIVE)

    def prepare(piece, j, first):
        spot = lax.broadcasted_iota(jnp.int32, (UNIT, HD), 0) + (piece * PIECE + j * UNIT)
        live = spot < prefix_len[row]
        rows = pl.ds(j * UNIT, UNIT)
        kx[...] = jnp.where(live, kv[piece, 0, rows].astype(F32), first.astype(F32)).astype(BF16)
        vx[:, 0:HD] = jnp.where(live, kv[piece, 1, rows].astype(F32), 0.0).astype(BF16)
        vx[:, HD:2 * HD] = jnp.where(live, 1.0, 0.0).astype(BF16)

    def update(h, keys, values, mask):
        scores = nt_dot(q[:, h * HD:(h + 1) * HD], keys)
        if mask is not None:
            scores = scores + mask
        old = m_ref[h]
        new = jnp.maximum(old, jnp.max(scores, 1, keepdims=True))
        expon = jnp.exp2((scores - new[:, 0:1]) * (SCALE * LOG2E)).astype(BF16)
        rescale = jnp.exp2((old - new) * (SCALE * LOG2E))
        m_ref[h] = new
        acc_ref[h] = acc_ref[h] * jnp.concatenate([rescale, rescale], 1) + jnp.dot(
            expon, values, preferred_element_type=F32
        )

    def forget_dead():
        m_ref[...] = jnp.where(ctx * PIECE < prefix_len[row], m_ref[...], NEGATIVE)

    def first_unit(j):
        prepare(ctx, j, kv[ctx, 0, 0:1, :])
        for h in range(GROUP):
            update(h, kx[...], vx[...], None)

    def unit(piece, j):
        prepare(piece, j, k0[0, 0:1, :])
        for h in range(GROUP):
            update(h, kx[...], vx[...], None)

    def span_unit():
        for i in range(4):
            kx[pl.ds(i * 256, 256)] = span[i % 2, x, i // 2 * 2 + y_lo, 0]
            vx[pl.ds(i * 256, 256), 0:HD] = span[i % 2, x, i // 2 * 2 + y_lo, 1]
        vx[:, HD:2 * HD] = jnp.ones((SPAN, HD), BF16)

        for h in range(GROUP):
            update(h, kx[...], vx[...], span_bias[...])

    def prefill_end():
        for h in range(GROUP):
            acc = acc_ref[h]
            pre_out[:, h * HD:(h + 1) * HD] = (acc[:, 0:HD] / acc[:, HD:2 * HD]).astype(BF16)

    for i in (2, 3, 6):
        locals_[i].wait()
    prefill_start()
    first_unit(0)
    for i in (0, 4, 5, 10):
        locals_[i].wait()
    pl.semaphore_wait(barrier, 24)
    hidden_start(0)
    for c in k0_copies:
        c.start()
    span_open()
    prefix_core.start()
    first_unit(1)
    forget_dead()
    locals_[1].wait()
    hidden_wait(0)
    project(0)
    for c in k0_copies:
        c.wait()
    prefix_core.wait()
    scatter(0)
    span_relay()
    unit(other_ctx, 0)
    decode_bias()
    unit(other_ctx, 1)
    span_own_ready()
    span_unit()
    gather_rows(0)
    locals_[8].wait()
    locals_[9].wait()
    span_close()
    prefix_far_start(0, 2)
    attend_cache()
    span_done()
    pick_span()
    attend(0)
    locals_[7].wait()
    relay_attended(0)
    prefix_far_start(2, 8)
    out_project(0)
    finish_step(0)
    hidden_start(1)
    prefix_relay(0)
    unit(far_ctx, 0)
    hidden_wait(1)
    project(1)
    prefix_forward(0).wait()
    scatter(1)
    unit(diagonal_ctx, 0)
    prefix_relay(1)
    unit(far_ctx, 1)
    gather_rows(1)
    attend_cache()
    attend(1)
    prefix_forward(1).wait()
    unit(diagonal_ctx, 1)
    relay_attended(1)
    out_project(1)
    prefill_end()
    finish_step(1)


def local(
    prefill_query, prefix_keys, prefix_values, span_keys, span_values, prefix_len, context_len,
    hidden, qkv_weight, out_weight, cache_keys, cache_values, row_context, cache_len,
):
    dma = pltpu.SemaphoreType.DMA
    smem = pl.BlockSpec(memory_space=pltpu.SMEM)
    anywhere = pl.BlockSpec(memory_space=pl.ANY)
    vmem = pl.BlockSpec(memory_space=pltpu.VMEM)
    pre, steps = pl.pallas_call(
        kernel,
        out_shape=(
            jax.ShapeDtypeStruct((256, GROUP * HD), BF16),
            jax.ShapeDtypeStruct((STEPS, 32, 256), BF16),
        ),
        in_specs=[smem] * 4 + [anywhere] * 10,
        out_specs=(vmem, vmem),
        scratch_shapes=[
            pltpu.VMEM((256, GROUP * HD), BF16),
            pltpu.VMEM((4, 2, PIECE, HD), BF16),
            pltpu.VMEM((UNIT, HD), BF16),
            pltpu.VMEM((UNIT, 2 * HD), BF16),
            pltpu.VMEM((4, 16, HD), BF16),
            pltpu.VMEM((2, 4, 4, 2, 256, HD), BF16),
            pltpu.VMEM((DRW, KEYS, HD), BF16),
            pltpu.VMEM((DRW, KEYS, HD), BF16),
            pltpu.VMEM((DRW, GROUP, KEYS), F32),
            pltpu.VMEM((256, SPAN), F32),
            pltpu.VMEM((256, 1280), BF16),
            pltpu.VMEM((1024, 256), BF16),
            pltpu.VMEM((STEPS, 32, 256), BF16),
            pltpu.VMEM((STEPS, 8, 32, 256), BF16),
            pltpu.VMEM((STEPS, 2, 16, 16, 640), BF16),
            pltpu.VMEM((STEPS, 16, 16, 640), BF16),
            pltpu.VMEM((STEPS, 16, 16, 640), BF16),
            pltpu.VMEM((STEPS, 16, 16, 640), BF16),
            pltpu.VMEM((GROUP, DRW, HD), F32),
            pltpu.VMEM((STEPS, 2, DRW, HD), F32),
            pltpu.VMEM((DRW, GROUP, HD), F32),
            pltpu.VMEM((STEPS, 16, 512), BF16),
            pltpu.VMEM((STEPS, 2, 16, 16, 512), BF16),
            pltpu.VMEM((STEPS, 8, 32, 256), BF16),
            pltpu.VMEM((STEPS, 8, 32, 256), BF16),
            pltpu.VMEM((DRW, GROUP, KEYS - SPAN), F32),
            pltpu.VMEM((GROUP, 256, HD), F32),
            pltpu.VMEM((GROUP, 256, 2 * HD), F32),
            dma((11,)),
            dma((STEPS, 8)), dma((STEPS, 8)),
            dma((STEPS,)), dma((STEPS,)),
            dma((STEPS, 16)), dma((STEPS, 16)),
            dma((STEPS, 16)), dma((STEPS, 16)),
            dma((STEPS,)), dma((STEPS,)),
            dma((STEPS, 8)), dma((STEPS, 8)),
            dma((3,)), dma((3,)),
            dma((2, 4)), dma((2, 4)),
            dma((2, 4, 4)), dma((2, 4, 4)),
            dma((4, 4)), dma((4, 4)),
            dma, dma,
            dma((PIECE // CHUNK,)), dma((PIECE // CHUNK,)),
            dma((2,)), dma((2,)),
        ],
        compiler_params=pltpu.CompilerParams(
            collective_id=0, has_side_effects=True, vmem_limit_bytes=56 * 1024 * 1024
        ),
        name="layer",
    )(
        prefix_len, context_len, row_context, cache_len,
        prefill_query[0], prefix_keys[0], prefix_values[0], span_keys[0], span_values[0],
        hidden[None], qkv_weight.reshape(256, 1280), out_weight, cache_keys, cache_values,
    )
    return pre[None], steps


def solution(mesh):
    in_specs = (
        P("row", "ctx", "tp"),
        P("row", "ctx", "tp"),
        P("row", "ctx", "tp"),
        P("row", "ctx", "tp"),
        P("row", "ctx", "tp"),
        P(),
        P(),
        P("tp", ("ctx", "row")),
        P(("ctx", "row"), "tp", None),
        P("tp", ("ctx", "row")),
        P(("ctx", "row"), None, "tp"),
        P(("ctx", "row"), None, "tp"),
        P(),
        P(),
    )
    out_specs = (P("row", "ctx", "tp"), P(None, "tp", ("ctx", "row")))
    return jax.shard_map(local, mesh=mesh, in_specs=in_specs, out_specs=out_specs, check_vma=False)
```

profile of v0, /device:TPU:1, one launch (start us, length us, event | category | flops | bytes accessed | tf_op | source)
XLA Modules:
  0.0 93.7 jit_solution(5632983311983464018)
XLA Ops:
  0.6 89.9 %layer.1 = (bf16[256,1024]{1,0:T(8,128)(2,1)}, bf16[2,32,256]{2,1,0:T(8,128)(2,1)}) custom-call(s32[8]{0:T(128)} %prefix_len.1, s32[8]{0:T(128)} %context_len.1, s32[256]{0:T(256)} %row_context.1, s32[256]{0:T(256)} %cache_len.1, bf16[256,1024]{1,0:T(8,128)(2,1)} %bitcast.10, bf16[2048,128]{1,0:T(8,128)(2,1)} %bitcast.11, bf16[2048,128]{1,0:T(8,128)(2,1)} %bitcast.12, ...), custom_call_target="tpu_custom_call" | custom-call | tf_op jit(solution)/shard_map/layer/pallas_call | solution.py:482
  90.5 1.9 %copy.18 = bf16[1,256,1024]{2,1,0:T(8,128)(2,1)} copy(bf16[1,256,1024]{2,1,0:T(8,128)(2,1)} %bitcast.9) | data formatting | bytes 1048576
  92.4 1.4 %copy.19 = bf16[2,32,256]{2,1,0:T(8,128)(2,1)} copy(bf16[2,32,256]{2,1,0:T(8,128)(2,1)} %get-tuple-element.9) | data formatting | bytes 65536
where the time goes:
time: 94 us; the launch traced here: 93.7 us
  Pallas kernels  89.9 us (96%)
  local copies, waits for them, and re-layouts  3.24 us (3%)
    pallas_call x1, Pallas kernels, local(): pl.pallas_call(kernel, out_shape=(jax.ShapeDtypeStruct((256, GROUP * HD),...  89.9 us
    unnamed x2, local copies, waits for them, and re-layouts  3.24 us

commit v1 on v0

--- a/solution.py
+++ b/solution.py
@@ -22,6 +22,10 @@
 F32 = jnp.float32
 BF16 = jnp.bfloat16
 MESH = pl.DeviceIdType.MESH
+Z_ORDER = (4, 3, 5, 2, 6, 1, 7)
+PLANE_ORDER = (
+    (2, 2), (2, 1), (2, 3), (1, 2), (3, 2), (2, 0), (0, 2), (1, 1), (1, 3), (3, 1), (3, 3), (1, 0), (3, 0), (0, 1), (0, 3)
+)
 
 
 def nt_dot(a, b):
@@ -50,8 +54,8 @@
     me = y_hi * 8 + row
 
     def plane(e):
-        t = (me + e) % 16
-        return t, {"ctx": (t // 8) * 2 + core, "row": t % 8}
+        to_x, to_y = (x + e[0]) % 4, (y + e[1]) % 4
+        return (to_y // 2) * 8 + to_x * 2 + to_y % 2, {"ctx": (to_y // 2) * 2 + core, "row": to_x * 2 + to_y % 2}
 
     def along_y(e):
         t = (y + e) % 4
@@ -76,66 +80,56 @@
             src_ref=src, dst_ref=dst, send_sem=ssem, recv_sem=rsem, device_id=device, device_id_type=MESH
         )
 
+    barrier = pltpu.get_barrier_semaphore()
+
+    def greet(device):
+        pl.semaphore_signal(barrier, inc=1, device_id=device, device_id_type=MESH)
+
+    for e in Z_ORDER:
+        greet(along_z(e)[1])
+    for e in PLANE_ORDER:
+        greet(plane(e)[1])
+    greet(diagonal)
+    greet(other_core)
+
     locals_ = [
         (hid_hbm.at[0], state.at[0]),
-        (wq_hbm, wq),
+        (pk_hbm.at[pl.ds(0, 16)], k0.at[ctx]),
+        (sk_hbm, span.at[core, x, y, 0]),
+        (sv_hbm, span.at[core, x, y, 1]),
         (pk_hbm, kv.at[ctx, 0]),
         (pv_hbm, kv.at[ctx, 1]),
-        (sk_hbm, span.at[core, x, y, 0]),
-        (sv_hbm, span.at[core, x, y, 1]),
         (q_hbm, q),
-        (wo_hbm, wo),
+        (wq_hbm, wq),
         (ck_hbm, kd.at[:, pl.ds(SPAN, CACHE)]),
         (cv_hbm, vd.at[:, pl.ds(SPAN, CACHE)]),
-        (pk_hbm.at[pl.ds(0, 16)], k0.at[ctx]),
+        (wo_hbm, wo),
     ]
     locals_ = [pltpu.make_async_copy(a, b, local_sem.at[i]) for i, (a, b) in enumerate(locals_)]
     for c in locals_:
         c.start()
 
-    barrier = pltpu.get_barrier_semaphore()
-
-    def greet(device):
-        pl.semaphore_signal(barrier, inc=1, device_id=device, device_id_type=MESH)
-
-    def greet_plane(e, _):
-        greet(plane(e)[1])
-        return 0
-
-    def greet_z(e, _):
-        greet(along_z(e)[1])
-        return 0
-
-    lax.fori_loop(1, 16, greet_plane, 0)
-    lax.fori_loop(1, 8, greet_z, 0)
-    greet(other_core)
-    greet(diagonal)
-
     def hidden_copy(s, e):
         return remote(state.at[s], xall.at[s, tp], z_ssem.at[s, e], z_rsem.at[s, e], along_z(e)[1])
 
     def hidden_start(s):
-        def body(e, _):
+        for e in Z_ORDER:
             hidden_copy(s, e).start()
-            return 0
-        lax.fori_loop(1, 8, body, 0)
         xall[s, tp] = state[s]
 
     def hidden_wait(s):
-        def body(e, _):
+        for e in Z_ORDER:
             hidden_copy(s, e).wait()
-            return 0
-        lax.fori_loop(1, 8, body, 0)
 
     def pair_copy(s):
         return remote(part.at[s, 1 - core], pair.at[s], pr_ssem.at[s], pr_rsem.at[s], other_core)
 
     def rs_copy(s, e):
         t, device = plane(e)
-        return remote(rs_send.at[s, t], rs_recv.at[s, me], rs_ssem.at[s, e], rs_rsem.at[s, e], device)
+        return remote(rs_send.at[s, t], rs_recv.at[s, me], rs_ssem.at[s, e[0], e[1]], rs_rsem.at[s, e[0], e[1]], device)
 
     def att_copy(s, e):
-        return remote(att_send.at[s], att_all.at[s, core, me], at_ssem.at[s, e], at_rsem.at[s, e], plane(e)[1])
+        return remote(att_send.at[s], att_all.at[s, core, me], at_ssem.at[s, e[0], e[1]], at_rsem.at[s, e[0], e[1]], plane(e)[1])
 
     def att_forward(s):
         return remote(att_all.at[s, core], att_all.at[s, core], fw_ssem.at[s], fw_rsem.at[s], other_core)
@@ -156,13 +150,13 @@
             remote(piece, piece, s1_ssem.at[1, e], s1_rsem.at[1, e], along_y(e)),
         )
 
-    def span_second(d, e):
-        keys = span.at[core, (x + d) % 4, y, 0]
-        values = span.at[core, x, (y + d) % 4, 1]
-        return (
-            remote(keys, keys, s2_ssem.at[0, d, e], s2_rsem.at[0, d, e], along_y(e)),
-            remote(values, values, s2_ssem.at[1, d, e], s2_rsem.at[1, d, e], along_x(e)),
-        )
+    def keys_on(d, e):
+        piece = span.at[core, (x + d) % 4, y, 0]
+        return remote(piece, piece, s2_ssem.at[0, d, e], s2_rsem.at[0, d, e], along_y(e))
+
+    def values_on(d, e):
+        piece = span.at[core, x, (y + d) % 4, 1]
+        return remote(piece, piece, s2_ssem.at[1, d, e], s2_rsem.at[1, d, e], along_x(e))
 
     def span_core(d, e):
         piece = span.at[core, (x + d) % 4, (y + e) % 4]
@@ -174,35 +168,28 @@
                 c.start()
         span_core(0, 0).start()
 
-    def span_relay():
-        for d in (1, 3, 2):
+    def span_relay(*which):
+        for d in which:
             along, across = span_first(d)
             along.wait()
             across.wait()
             for e in (1, 3, 2):
-                for c in span_second(4 - d, e):
-                    c.start()
+                keys_on(4 - d, e).start()
+                values_on(4 - d, e).start()
             span_core(4 - d, 0).start()
             span_core(0, 4 - d).start()
 
-    def span_own_ready():
-        span_core(0, 0).wait()
-        span_core(0, 2).wait()
-
     def span_close():
-        for d in (1, 3, 2):
-            for e in (1, 3, 2):
-                for c in span_second(d, e):
-                    c.wait()
-        for d in (1, 2, 3):
-            for e in (1, 2, 3):
-                span_core(d, e).start()
+        for a in (3, 1, 2):
+            for b in (3, 1, 2):
+                keys_on(a, 4 - b).wait()
+                values_on(b, 4 - a).wait()
+                span_core(a, b).start()
 
     def span_done():
         for d in range(4):
             for e in range(4):
-                if (d, e) not in ((0, 0), (0, 2)):
-                    span_core(d, e).wait()
+                span_core(d, e).wait()
 
     prefix_core = remote(kv.at[ctx], kv.at[ctx], pc_ssem, pc_rsem, other_core)
 
@@ -224,28 +211,27 @@
             prefix_far(i).wait()
         prefix_forward(j).start()
 
+    def project_rows(s, c):
+        rows = jnp.concatenate([xall[s, pl.ds(c * 2, 2)], xall[s, pl.ds(4 + c * 2, 2)]], 0).reshape(128, 256)
+        out = jnp.dot(rows, wq[...], preferred_element_type=F32).reshape(16, 8, 1280)
+        part[s, c] = jnp.concatenate([out[:, :, :640], out[:, :, 640:]], 1).astype(BF16)
+
     def project(s):
-        out = jnp.dot(xall[s].reshape(256, 256), wq[...], preferred_element_type=F32).reshape(32, 8, 1280)
-        both = jnp.concatenate([out[:, :, :640], out[:, :, 640:]], 1).astype(BF16)
-        for j in range(4):
-            part[s, j % 2, pl.ds((j // 2) * 8, 8)] = both[j * 8:j * 8 + 8]
+        project_rows(s, 1 - core)
         pair_copy(s).start()
+        project_rows(s, core)
 
     def scatter(s):
         pair_copy(s).wait()
         rs_send[s] = (part[s, core].astype(F32) + pair[s].astype(F32)).astype(BF16)
 
-        def body(e, _):
+        for e in PLANE_ORDER:
             rs_copy(s, e).start()
-            return 0
-        lax.fori_loop(1, 16, body, 0)
         rs_recv[s, me] = rs_send[s, me]
 
     def gather_rows(s):
-        def body(e, _):
+        for e in PLANE_ORDER:
             rs_copy(s, e).wait()
-            return 0
-        lax.fori_loop(1, 16, body, 0)
         total = jnp.sum(rs_recv[s].astype(F32), 0).astype(BF16).astype(F32)
         for i in range(5):
             heads[i] = total[0:8, i * HD:(i + 1) * HD]
@@ -288,39 +274,34 @@
             both = jnp.concatenate([att_o[:, i, :], att_o[:, 4 + i, :]], 0)
             att_send[s, :, i * HD:(i + 1) * HD] = both.astype(BF16)
 
-        def body(e, _):
+        for e in PLANE_ORDER:
             att_copy(s, e).start()
-            return 0
-        lax.fori_loop(1, 16, body, 0)
         att_all[s, core, me] = att_send[s]
 
     def relay_attended(s):
-        def body(e, _):
+        for e in PLANE_ORDER:
             att_copy(s, e).wait()
-            return 0
-        lax.fori_loop(1, 16, body, 0)
         att_forward(s).start()
 
-    def out_project(s):
-        att_forward(s).wait()
-        rows = att_all[s].astype(F32).reshape(32, 16, 512)
-        left = rows[:, 0:8].reshape(256, 512).astype(BF16)
-        right = rows[:, 8:16].reshape(256, 512).astype(BF16)
+    def out_project_rows(s, c):
+        rows = att_all[s, c].astype(F32)
+        left = rows[:, 0:8].reshape(128, 512).astype(BF16)
+        right = rows[:, 8:16].reshape(128, 512).astype(BF16)
         out = jnp.dot(left, wo[0:512], preferred_element_type=F32)
         out = out + jnp.dot(right, wo[512:1024], preferred_element_type=F32)
-        z_send[s] = out.astype(BF16).reshape(8, 32, 256)
-
-        def body(e, _):
+        z_send[s, pl.ds(c * 4, 4)] = out.astype(BF16).reshape(4, 32, 256)
+
+    def out_project(s):
+        out_project_rows(s, core)
+        att_forward(s).wait()
+        out_project_rows(s, 1 - core)
+        for e in Z_ORDER:
             out_copy(s, e).start()
-            return 0
-        lax.fori_loop(1, 8, body, 0)
         z_recv[s, tp] = z_send[s, ((tp // 2) % 2 * 2 + tp // 4) * 2 + tp % 2]
 
     def finish_step(s):
-        def body(e, _):
+        for e in Z_ORDER:
             out_copy(s, e).wait()
-            return 0
-        lax.fori_loop(1, 8, body, 0)
         result = jnp.sum(z_recv[s].astype(F32), 0).astype(BF16)
         step_out[s] = result
         if s + 1 < STEPS:
@@ -409,45 +390,43 @@
             acc = acc_ref[h]
             pre_out[:, h * HD:(h + 1) * HD] = (acc[:, 0:HD] / acc[:, HD:2 * HD]).astype(BF16)
 
-    for i in (2, 3, 6):
-        locals_[i].wait()
-    prefill_start()
-    first_unit(0)
-    for i in (0, 4, 5, 10):
+    for i in range(4):
         locals_[i].wait()
     pl.semaphore_wait(barrier, 24)
     hidden_start(0)
     for c in k0_copies:
         c.start()
     span_open()
+    for i in range(4, 7):
+        locals_[i].wait()
     prefix_core.start()
+    prefill_start()
+    first_unit(0)
+    locals_[7].wait()
+    hidden_wait(0)
+    project(0)
+    span_relay(1, 3)
+    scatter(0)
+    span_relay(2)
     first_unit(1)
     forget_dead()
-    locals_[1].wait()
-    hidden_wait(0)
-    project(0)
     for c in k0_copies:
         c.wait()
     prefix_core.wait()
-    scatter(0)
-    span_relay()
     unit(other_ctx, 0)
     decode_bias()
-    unit(other_ctx, 1)
-    span_own_ready()
-    span_unit()
+    for i in range(8, 11):
+        locals_[i].wait()
+    span_close()
     gather_rows(0)
-    locals_[8].wait()
-    locals_[9].wait()
-    span_close()
     prefix_far_start(0, 2)
     attend_cache()
     span_done()
     pick_span()
     attend(0)
-    locals_[7].wait()
+    unit(other_ctx, 1)
     relay_attended(0)
-    prefix_far_start(2, 8)
+    prefix_far_start(2, 7)
     out_project(0)
     finish_step(0)
     hidden_start(1)
@@ -458,17 +437,24 @@
     prefix_forward(0).wait()
     scatter(1)
     unit(diagonal_ctx, 0)
-    prefix_relay(1)
-    unit(far_ctx, 1)
     gather_rows(1)
+    prefix_far_start(7, 8)
     attend_cache()
     attend(1)
+    span_unit()
+    relay_attended(1)
+    prefix_relay(1)
+    out_project(1)
+    unit(far_ctx, 1)
     prefix_forward(1).wait()
     unit(diagonal_ctx, 1)
-    relay_attended(1)
-    out_project(1)
     prefill_end()
     finish_step(1)
+
+
+def hand_on(pre, steps, pre_out, steps_out):
+    pre_out[0] = pre[...]
+    steps_out[...] = steps[...]
 
 
 def local(
@@ -519,8 +505,8 @@
             dma((11,)),
             dma((STEPS, 8)), dma((STEPS, 8)),
             dma((STEPS,)), dma((STEPS,)),
-            dma((STEPS, 16)), dma((STEPS, 16)),
-            dma((STEPS, 16)), dma((STEPS, 16)),
+            dma((STEPS, 4, 4)), dma((STEPS, 4, 4)),
+            dma((STEPS, 4, 4)), dma((STEPS, 4, 4)),
             dma((STEPS,)), dma((STEPS,)),
             dma((STEPS, 8)), dma((STEPS, 8)),
             dma((3,)), dma((3,)),
@@ -540,7 +526,16 @@
         prefill_query[0], prefix_keys[0], prefix_values[0], span_keys[0], span_values[0],
         hidden[None], qkv_weight.reshape(256, 1280), out_weight, cache_keys, cache_values,
     )
-    return pre[None], steps
+    return pl.pallas_call(
+        hand_on,
+        out_shape=(
+            jax.ShapeDtypeStruct((1, 256, GROUP * HD), BF16),
+            jax.ShapeDtypeStruct((STEPS, 32, 256), BF16),
+        ),
+        in_specs=[vmem, vmem],
+        out_specs=(vmem, vmem),
+        name="hand_on",
+    )(pre, steps)
 
 
 def solution(mesh):

time: 94 us -> 85.4 us (0.909)
  Pallas kernels: 89.9 us -> 84.6 us
  local copies, waits for them, and re-layouts: 3.24 us -> 0 us
    pallas_call x1, Pallas kernels: 89.9 us -> 82.7 us  [local(): pl.pallas_call(kernel, out_shape=(jax.ShapeDtypeStruct((256, GROUP * HD),...]
    unnamed x2 -> x0, local copies, waits for them, and re-layouts: 3.24 us -> none
    pallas_call x0 -> x1, Pallas kernels: none -> 1.87 us  [local(): pl.pallas_call(hand_on, out_shape=(jax.ShapeDtypeStruct((1, 256, GROUP *...]
where the time goes in v1:
time: 85.4 us; the launch traced here: 85.2 us
  Pallas kernels  84.6 us (99%)
    pallas_call x1, Pallas kernels, local(): pl.pallas_call(kernel, out_shape=(jax.ShapeDtypeStruct((256, GROUP * HD),...  82.7 us
    pallas_call x1, Pallas kernels, local(): pl.pallas_call(hand_on, out_shape=(jax.ShapeDtypeStruct((1, 256, GROUP *...  1.87 us

profile of v1, /device:TPU:1, one launch (start us, length us, event | category | flops | bytes accessed | tf_op | source)
XLA Modules:
  0.0 85.2 jit_solution(12556614625088023538)
XLA Ops:
  0.6 82.7 %layer.1 = (bf16[256,1024]{1,0:T(8,128)(2,1)}, bf16[2,32,256]{2,1,0:T(8,128)(2,1)}) custom-call(s32[8]{0:T(128)} %prefix_len.1, s32[8]{0:T(128)} %context_len.1, s32[256]{0:T(256)} %row_context.1, s32[256]{0:T(256)} %cache_len.1, bf16[256,1024]{1,0:T(8,128)(2,1)} %bitcast.8, bf16[2048,128]{1,0:T(8,128)(2,1)} %bitcast.9, bf16[2048,128]{1,0:T(8,128)(2,1)} %bitcast.10, ...), custom_call_target="tpu_custom_call" | custom-call | tf_op jit(solution)/shard_map/layer/pallas_call | solution.py:468
  83.4 1.9 %hand_on.1 = (bf16[1,256,1024]{2,1,0:T(8,128)(2,1)}, bf16[2,32,256]{2,1,0:T(8,128)(2,1)}) custom-call(bf16[256,1024]{1,0:T(8,128)(2,1)} %get-tuple-element.4.pre, bf16[2,32,256]{2,1,0:T(8,128)(2,1)} %get-tuple-element.5.steps), custom_call_target="tpu_custom_call" | custom-call | tf_op jit(solution)/shard_map/hand_on/pallas_call | solution.py:529

commit v2 on v1

--- a/solution.py
+++ b/solution.py
@@ -33,10 +33,10 @@
 
 
 def kernel(
-    prefix_len, context_len, row_context, cache_len,
+    prefix_len_any, context_len_any, row_context_any, cache_len_any,
     q_hbm, pk_hbm, pv_hbm, sk_hbm, sv_hbm, hid_hbm, wq_hbm, wo_hbm, ck_hbm, cv_hbm,
-    pre_out, step_out,
-    q, kv, kx, vx, k0, span, kd, vd, bias, span_bias, wq, wo,
+    pre_any, step_any,
+    prefix_len, context_len, row_context, cache_len, pre_out, step_out, q, kv, kx, vx, k0, span, kd, vd, bias, span_bias, wq, wo,
     state, xall, part, pair, rs_send, rs_recv, heads, new_kv, att_o, att_send, att_all, z_send, z_recv, late,
     m_ref, acc_ref,
     local_sem, z_ssem, z_rsem, pr_ssem, pr_rsem, rs_ssem, rs_rsem, at_ssem, at_rsem, fw_ssem, fw_rsem,
@@ -75,6 +75,9 @@
     far_ctx = (1 - y_hi) * 2 + core
     diagonal_ctx = (1 - y_hi) * 2 + 1 - core
 
+    def wait_bytes(ref, sem):
+        pltpu.make_async_copy(ref, ref, sem).wait()
+
     def remote(src, dst, ssem, rsem, device):
         return pltpu.make_async_remote_copy(
             src_ref=src, dst_ref=dst, send_sem=ssem, recv_sem=rsem, device_id=device, device_id_type=MESH
@@ -104,13 +107,22 @@
         (ck_hbm, kd.at[:, pl.ds(SPAN, CACHE)]),
         (cv_hbm, vd.at[:, pl.ds(SPAN, CACHE)]),
         (wo_hbm, wo),
+        (prefix_len_any, prefix_len),
+        (context_len_any, context_len),
+        (row_context_any, row_context),
+        (cache_len_any, cache_len),
     ]
     locals_ = [pltpu.make_async_copy(a, b, local_sem.at[i]) for i, (a, b) in enumerate(locals_)]
     for c in locals_:
         c.start()
+    results = [
+        pltpu.make_async_copy(step_out.at[0], step_any.at[0], local_sem.at[15]),
+        pltpu.make_async_copy(step_out.at[1], step_any.at[1], local_sem.at[16]),
+        pltpu.make_async_copy(pre_out, pre_any, local_sem.at[17]),
+    ]
 
     def hidden_copy(s, e):
-        return remote(state.at[s], xall.at[s, tp], z_ssem.at[s, e], z_rsem.at[s, e], along_z(e)[1])
+        return remote(state.at[s], xall.at[s, tp], z_ssem.at[s], z_rsem.at[s], along_z(e)[1])
 
     def hidden_start(s):
         for e in Z_ORDER:
@@ -118,18 +130,18 @@
         xall[s, tp] = state[s]
 
     def hidden_wait(s):
-        for e in Z_ORDER:
-            hidden_copy(s, e).wait()
+        wait_bytes(xall.at[s, pl.ds(0, 7)], z_ssem.at[s])
+        wait_bytes(xall.at[s, pl.ds(0, 7)], z_rsem.at[s])
 
     def pair_copy(s):
         return remote(part.at[s, 1 - core], pair.at[s], pr_ssem.at[s], pr_rsem.at[s], other_core)
 
     def rs_copy(s, e):
         t, device = plane(e)
-        return remote(rs_send.at[s, t], rs_recv.at[s, me], rs_ssem.at[s, e[0], e[1]], rs_rsem.at[s, e[0], e[1]], device)
+        return remote(rs_send.at[s, t], rs_recv.at[s, me], rs_ssem.at[s], rs_rsem.at[s], device)
 
     def att_copy(s, e):
-        return remote(att_send.at[s], att_all.at[s, core, me], at_ssem.at[s, e[0], e[1]], at_rsem.at[s, e[0], e[1]], plane(e)[1])
+        return remote(att_send.at[s], att_all.at[s, core, me], at_ssem.at[s], at_rsem.at[s], plane(e)[1])
 
     def att_forward(s):
         return remote(att_all.at[s, core], att_all.at[s, core], fw_ssem.at[s], fw_rsem.at[s], other_core)
@@ -137,30 +149,30 @@
     def out_copy(s, e):
         t, device = along_z(e)
         block = ((t // 2) % 2 * 2 + t // 4) * 2 + t % 2
-        return remote(z_send.at[s, block], z_recv.at[s, tp], rz_ssem.at[s, e], rz_rsem.at[s, e], device)
+        return remote(z_send.at[s, block], z_recv.at[s, tp], rz_ssem.at[s], rz_rsem.at[s], device)
 
     k0_copies = [
-        remote(k0.at[ctx], k0.at[ctx], k0_ssem.at[i], k0_rsem.at[i], device)
-        for i, device in enumerate((other_core, far, diagonal))
+        remote(k0.at[ctx], k0.at[ctx], k0_ssem, k0_rsem, device)
+        for device in (other_core, far, diagonal)
     ]
     def span_first(e):
         piece = span.at[core, x, y]
         return (
-            remote(piece, piece, s1_ssem.at[0, e], s1_rsem.at[0, e], along_x(e)),
-            remote(piece, piece, s1_ssem.at[1, e], s1_rsem.at[1, e], along_y(e)),
+            remote(piece, piece, s1_ssem.at[0, e - 1], s1_rsem.at[0, e - 1], along_x(e)),
+            remote(piece, piece, s1_ssem.at[1, e - 1], s1_rsem.at[1, e - 1], along_y(e)),
         )
 
     def keys_on(d, e):
         piece = span.at[core, (x + d) % 4, y, 0]
-        return remote(piece, piece, s2_ssem.at[0, d, e], s2_rsem.at[0, d, e], along_y(e))
+        return remote(piece, piece, s2_ssem.at[0, d - 1, e - 1], s2_rsem.at[0, d - 1, e - 1], along_y(e))
 
     def values_on(d, e):
         piece = span.at[core, x, (y + d) % 4, 1]
-        return remote(piece, piece, s2_ssem.at[1, d, e], s2_rsem.at[1, d, e], along_x(e))
+        return remote(piece, piece, s2_ssem.at[1, d - 1, e - 1], s2_rsem.at[1, d - 1, e - 1], along_x(e))
 
     def span_core(d, e):
         piece = span.at[core, (x + d) % 4, (y + e) % 4]
-        return remote(piece, piece, sf_ssem.at[d, e], sf_rsem.at[d, e], other_core)
+        return remote(piece, piece, sf_ssem, sf_rsem, other_core)
 
     def span_open():
         for e in (1, 3, 2):
@@ -187,9 +199,8 @@
                 span_core(a, b).start()
 
     def span_done():
-        for d in range(4):
-            for e in range(4):
-                span_core(d, e).wait()
+        wait_bytes(span.at[core], sf_ssem)
+        wait_bytes(span.at[1 - core], sf_rsem)
 
     prefix_core = remote(kv.at[ctx], kv.at[ctx], pc_ssem, pc_rsem, other_core)
 
@@ -201,13 +212,15 @@
         for i in range(first, last):
             prefix_far(i).start()
 
+    onward = ((0, 4), (4, 7), (7, 8))
+
     def prefix_forward(j):
-        half = kv.at[far_ctx, :, pl.ds(j * UNIT, UNIT)]
-        return remote(half, half, pd_ssem.at[j], pd_rsem.at[j], other_core)
+        first, last = onward[j]
+        rows = kv.at[far_ctx, :, pl.ds(first * CHUNK, (last - first) * CHUNK)]
+        return remote(rows, rows, pd_ssem.at[j], pd_rsem.at[j], other_core)
 
     def prefix_relay(j):
-        per = UNIT // CHUNK
-        for i in range(j * per, (j + 1) * per):
+        for i in range(*onward[j]):
             prefix_far(i).wait()
         prefix_forward(j).start()
 
@@ -230,8 +243,8 @@
         rs_recv[s, me] = rs_send[s, me]
 
     def gather_rows(s):
-        for e in PLANE_ORDER:
-            rs_copy(s, e).wait()
+        wait_bytes(rs_recv.at[s, pl.ds(0, 15)], rs_ssem.at[s])
+        wait_bytes(rs_recv.at[s, pl.ds(0, 15)], rs_rsem.at[s])
         total = jnp.sum(rs_recv[s].astype(F32), 0).astype(BF16).astype(F32)
         for i in range(5):
             heads[i] = total[0:8, i * HD:(i + 1) * HD]
@@ -279,8 +292,8 @@
         att_all[s, core, me] = att_send[s]
 
     def relay_attended(s):
-        for e in PLANE_ORDER:
-            att_copy(s, e).wait()
+        wait_bytes(att_all.at[s, core, pl.ds(0, 15)], at_ssem.at[s])
+        wait_bytes(att_all.at[s, core, pl.ds(0, 15)], at_rsem.at[s])
         att_forward(s).start()
 
     def out_project_rows(s, c):
@@ -300,8 +313,8 @@
         z_recv[s, tp] = z_send[s, ((tp // 2) % 2 * 2 + tp // 4) * 2 + tp % 2]
 
     def finish_step(s):
-        for e in Z_ORDER:
-            out_copy(s, e).wait()
+        wait_bytes(z_recv.at[s, pl.ds(0, 7)], rz_ssem.at[s])
+        wait_bytes(z_recv.at[s, pl.ds(0, 7)], rz_rsem.at[s])
         result = jnp.sum(z_recv[s].astype(F32), 0).astype(BF16)
         step_out[s] = result
         if s + 1 < STEPS:
@@ -342,13 +355,15 @@
         valid = context_len[row] - prefix_len[row]
         span_bias[...] = jnp.where((spot <= at) & (spot < valid), 0.0, NEGATIVE)
 
-    def prepare(piece, j, first):
-        spot = lax.broadcasted_iota(jnp.int32, (UNIT, HD), 0) + (piece * PIECE + j * UNIT)
-        live = spot < prefix_len[row]
-        rows = pl.ds(j * UNIT, UNIT)
-        kx[...] = jnp.where(live, kv[piece, 0, rows].astype(F32), first.astype(F32)).astype(BF16)
-        vx[:, 0:HD] = jnp.where(live, kv[piece, 1, rows].astype(F32), 0.0).astype(BF16)
-        vx[:, HD:2 * HD] = jnp.where(live, 1.0, 0.0).astype(BF16)
+    def prepare(blocks, first):
+        at = 0
+        for piece, start, n in blocks:
+            live = lax.broadcasted_iota(jnp.int32, (n, HD), 0) + (piece * PIECE + start) < prefix_len[row]
+            rows, to = pl.ds(start, n), pl.ds(at, n)
+            kx[to] = jnp.where(live, kv[piece, 0, rows].astype(F32), first.astype(F32)).astype(BF16)
+            vx[to, 0:HD] = jnp.where(live, kv[piece, 1, rows].astype(F32), 0.0).astype(BF16)
+            vx[to, HD:2 * HD] = jnp.where(live, 1.0, 0.0).astype(BF16)
+            at += n
 
     def update(h, keys, values, mask):
         scores = nt_dot(q[:, h * HD:(h + 1) * HD], keys)
@@ -367,12 +382,12 @@
         m_ref[...] = jnp.where(ctx * PIECE < prefix_len[row], m_ref[...], NEGATIVE)
 
     def first_unit(j):
-        prepare(ctx, j, kv[ctx, 0, 0:1, :])
+        prepare([(ctx, j * UNIT, UNIT)], kv[ctx, 0, 0:1, :])
         for h in range(GROUP):
             update(h, kx[...], vx[...], None)
 
-    def unit(piece, j):
-        prepare(piece, j, k0[0, 0:1, :])
+    def unit(*blocks):
+        prepare(blocks, k0[0, 0:1, :])
         for h in range(GROUP):
             update(h, kx[...], vx[...], None)
 
@@ -397,7 +412,7 @@
     for c in k0_copies:
         c.start()
     span_open()
-    for i in range(4, 7):
+    for i in (4, 5, 6, 11, 12, 13, 14):
         locals_[i].wait()
     prefix_core.start()
     prefill_start()
@@ -410,10 +425,10 @@
     span_relay(2)
     first_unit(1)
     forget_dead()
-    for c in k0_copies:
-        c.wait()
+    wait_bytes(k0.at[pl.ds(0, 3)], k0_ssem)
+    wait_bytes(k0.at[pl.ds(0, 3)], k0_rsem)
     prefix_core.wait()
-    unit(other_ctx, 0)
+    unit((other_ctx, 0, UNIT))
     decode_bias()
     for i in range(8, 11):
         locals_[i].wait()
@@ -424,32 +439,39 @@
     span_done()
     pick_span()
     attend(0)
-    unit(other_ctx, 1)
+    unit((other_ctx, UNIT, UNIT))
     relay_attended(0)
     prefix_far_start(2, 7)
     out_project(0)
+    span_unit()
     finish_step(0)
+    results[0].start()
     hidden_start(1)
     prefix_relay(0)
-    unit(far_ctx, 0)
+    unit((far_ctx, 0, UNIT))
     hidden_wait(1)
     project(1)
     prefix_forward(0).wait()
     scatter(1)
-    unit(diagonal_ctx, 0)
+    unit((diagonal_ctx, 0, UNIT))
+    prefix_relay(1)
     gather_rows(1)
     prefix_far_start(7, 8)
     attend_cache()
     attend(1)
-    span_unit()
+    prefix_forward(1).wait()
+    unit((far_ctx, 4 * CHUNK, 3 * CHUNK), (diagonal_ctx, 4 * CHUNK, CHUNK))
     relay_attended(1)
-    prefix_relay(1)
+    prefix_relay(2)
     out_project(1)
-    unit(far_ctx, 1)
-    prefix_forward(1).wait()
-    unit(diagonal_ctx, 1)
+    prefix_forward(2).wait()
+    unit((far_ctx, 7 * CHUNK, CHUNK), (diagonal_ctx, 5 * CHUNK, 3 * CHUNK))
     prefill_end()
+    results[2].start()
     finish_step(1)
+    results[1].start()
+    for c in results:
+        c.wait()
 
 
 def hand_on(pre, steps, pre_out, steps_out):
@@ -462,7 +484,6 @@
     hidden, qkv_weight, out_weight, cache_keys, cache_values, row_context, cache_len,
 ):
     dma = pltpu.SemaphoreType.DMA
-    smem = pl.BlockSpec(memory_space=pltpu.SMEM)
     anywhere = pl.BlockSpec(memory_space=pl.ANY)
     vmem = pl.BlockSpec(memory_space=pltpu.VMEM)
     pre, steps = pl.pallas_call(
@@ -471,9 +492,15 @@
             jax.ShapeDtypeStruct((256, GROUP * HD), BF16),
             jax.ShapeDtypeStruct((STEPS, 32, 256), BF16),
         ),
-        in_specs=[smem] * 4 + [anywhere] * 10,
-        out_specs=(vmem, vmem),
+        in_specs=[anywhere] * 14,
+        out_specs=(anywhere, anywhere),
         scratch_shapes=[
+            pltpu.SMEM((8,), jnp.int32),
+            pltpu.SMEM((8,), jnp.int32),
+            pltpu.SMEM((256,), jnp.int32),
+            pltpu.SMEM((256,), jnp.int32),
+            pltpu.VMEM((256, GROUP * HD), BF16),
+            pltpu.VMEM((STEPS, 32, 256), BF16),
             pltpu.VMEM((256, GROUP * HD), BF16),
             pltpu.VMEM((4, 2, PIECE, HD), BF16),
             pltpu.VMEM((UNIT, HD), BF16),
@@ -502,20 +529,20 @@
             pltpu.VMEM((DRW, GROUP, KEYS - SPAN), F32),
             pltpu.VMEM((GROUP, 256, HD), F32),
             pltpu.VMEM((GROUP, 256, 2 * HD), F32),
-            dma((11,)),
-            dma((STEPS, 8)), dma((STEPS, 8)),
+            dma((18,)),
             dma((STEPS,)), dma((STEPS,)),
-            dma((STEPS, 4, 4)), dma((STEPS, 4, 4)),
-            dma((STEPS, 4, 4)), dma((STEPS, 4, 4)),
             dma((STEPS,)), dma((STEPS,)),
-            dma((STEPS, 8)), dma((STEPS, 8)),
-            dma((3,)), dma((3,)),
-            dma((2, 4)), dma((2, 4)),
-            dma((2, 4, 4)), dma((2, 4, 4)),
-            dma((4, 4)), dma((4, 4)),
+            dma((STEPS,)), dma((STEPS,)),
+            dma((STEPS,)), dma((STEPS,)),
+            dma((STEPS,)), dma((STEPS,)),
+            dma((STEPS,)), dma((STEPS,)),
+            dma, dma,
+            dma((2, 3)), dma((2, 3)),
+            dma((2, 3, 3)), dma((2, 3, 3)),
+            dma, dma,
             dma, dma,
             dma((PIECE // CHUNK,)), dma((PIECE // CHUNK,)),
-            dma((2,)), dma((2,)),
+            dma((3,)), dma((3,)),
         ],
         compiler_params=pltpu.CompilerParams(
             collective_id=0, has_side_effects=True, vmem_limit_bytes=56 * 1024 * 1024

time: 85.4 us -> 80.8 us (0.946)
  Pallas kernels: 84.6 us -> 80 us
    pallas_call x1, Pallas kernels: 82.7 us -> 78.2 us  [local(): pl.pallas_call(kernel, out_shape=(jax.ShapeDtypeStruct((256, GROUP * HD),...]
where the time goes in v2:
time: 80.8 us; the launch traced here: 80.7 us
  Pallas kernels  80 us (99%)
    pallas_call x1, Pallas kernels, local(): pl.pallas_call(kernel, out_shape=(jax.ShapeDtypeStruct((256, GROUP * HD),...  78.2 us
    pallas_call x1, Pallas kernels, local(): pl.pallas_call(hand_on, out_shape=(jax.ShapeDtypeStruct((1, 256, GROUP *...  1.87 us

profile of v2, /device:TPU:1, one launch (start us, length us, event | category | flops | bytes accessed | tf_op | source)
XLA Modules:
  0.0 80.7 jit_solution(14356219355445174328)
XLA Ops:
  0.6 78.2 %layer.1 = (bf16[256,1024]{1,0:T(8,128)(2,1)}, bf16[2,32,256]{2,1,0:T(8,128)(2,1)}) custom-call(s32[8]{0:T(128)} %prefix_len_any.1, s32[8]{0:T(128)} %context_len_any.1, s32[256]{0:T(256)} %row_context_any.1, s32[256]{0:T(256)} %cache_len_any.1, bf16[256,1024]{1,0:T(8,128)(2,1)} %bitcast.8, bf16[2048,128]{1,0:T(8,128)(2,1)} %bitcast.9, ...), custom_call_target="tpu_custom_call" | custom-call | tf_op jit(solution)/shard_map/layer/pallas_call | solution.py:489
  78.8 1.9 %hand_on.1 = (bf16[1,256,1024]{2,1,0:T(8,128)(2,1)}, bf16[2,32,256]{2,1,0:T(8,128)(2,1)}) custom-call(bf16[256,1024]{1,0:T(8,128)(2,1)} %get-tuple-element.4.pre, bf16[2,32,256]{2,1,0:T(8,128)(2,1)} %get-tuple-element.5.steps), custom_call_target="tpu_custom_call" | custom-call | tf_op jit(solution)/shard_map/hand_on/pallas_call | solution.py:556
